TPU v7x, 32 devices: a whole 2x2x4 slice. The times are simulated.
32 devices in a mesh: row: 4 (over y, core), col: 2 (over x), fib: 4 (over z).
Axes of the slice: x: 2, y: 2, z: 4, core: 2. Of those that a mesh axis runs over, the one named last changes fastest.
Arguments:
- values: bfloat16 [48, 12, 128, 128], P(('row', 'col'), 'fib'), may hold values from -3 to 3
- columns: int32 [48, 12], P(('row', 'col')), may hold values from 0 to 47, as said below
- counts: int32 [48], P(('row', 'col')), may hold values from 6 to 12, as said below
Outputs:
- square: bfloat16 [48, 12, 128, 128], P(('row', 'col'), 'fib')
- traces: float32 [2], replicated
Inputs may be any that keep to these rules, and one draw needn't show every extreme that they name: Slot 0 of block row i holds i. Every slot s >= 1 of row i, used or not, holds (i + o) mod 48 with 1 <= |o| <= 6, and the columns of one row are distinct. Row i uses slots 0 to counts[i] - 1; later slots are ignored. Some row uses all 12 slots.
All inputs are finite; a program needn't handle non-finite values.
Results may differ from a plain program's by a relative error of at most 0.001.
Values may be sent and summed in bfloat16 or wider, within the bound.
No kernel may reach another device: no remote copies, remote signals or barrier semaphores. Data moves between devices by JAX's collectives and lax.ppermute only.
A program may use at most 128 MiB of HBM per device.

v0:
```python
import functools

import jax
import jax.numpy as jnp
from jax import lax
from jax.experimental import pallas as pl
from jax.experimental.pallas import tpu as pltpu
from jax.sharding import PartitionSpec as P

BAND = 6
PLANE = ("row", "col")
ALL = ("row", "col", "fib")
NT = (((1,), (1,)), ((), ()))


def padded(array, sides, width):
    for axis, dim in sides:
        size, length = (lax.axis_size(axis), array.shape[dim])
        up = [(i, (i + 1) % size) for i in range(size)]
        down = [(j, i) for i, j in up]
        last = lax.slice_in_dim(array, length - width, length, axis=dim)
        initial = lax.slice_in_dim(array, 0, width, axis=dim)
        before = lax.ppermute(last, axis, up)
        after = lax.ppermute(initial, axis, down)
        array = jnp.concatenate([before, array, after], axis=dim)
    return array


def band_product(
    left_tiles, left_keep, fetch_index, target_cols, target_keep, window, window_cols, window_counts
):
    picked = jnp.take(window, fetch_index, axis=0)
    picked_cols = jnp.take(window_cols, fetch_index, axis=0)
    picked_counts = jnp.take(window_counts, fetch_index, axis=0)
    alive_slots = lax.broadcasted_iota(jnp.int32, picked_cols.shape, 1) < picked_counts[:, None]
    matches = (picked_cols[:, None, :] == target_cols[None, :, None]) & alive_slots[:, None, :]
    matches = matches & left_keep[:, None, None] & target_keep[None, :, None]
    chosen = jnp.einsum(
        "ajs,asxy->ajxy", matches.astype(jnp.bfloat16), picked, preferred_element_type=jnp.float32
    ).astype(jnp.bfloat16)
    return jnp.einsum("axy,ajyz->jxz", left_tiles, chosen, preferred_element_type=jnp.float32)


def general_body(values, columns, counts):
    rows_here = values.shape[0]
    share_count = values.shape[1]
    slot_count = columns.shape[1]
    block_total = rows_here * lax.axis_size(("row", "col"))
    fib_index = lax.axis_index("fib")
    full_rows = lax.all_gather(values, "fib", axis=1, tiled=True)
    window, window_cols, window_counts = (
        padded(full_rows, ((("row", "col"), 0),), BAND),
        padded(columns, ((("row", "col"), 0),), BAND),
        padded(counts, ((("row", "col"), 0),), BAND),
    )
    local_rows = jnp.arange(rows_here, dtype=jnp.int32)
    row_ids = lax.axis_index(("row", "col")) * rows_here + local_rows
    fetch_all = (columns - row_ids[:, None] + BAND) % block_total + local_rows[:, None]
    slot_ids = jnp.arange(slot_count, dtype=jnp.int32)
    keep_mask = slot_ids[None, :] < counts[:, None]
    first_slot = fib_index * share_count

    def one_row(operands):
        return band_product(*operands, window, window_cols, window_counts)

    own_rows = lax.dynamic_slice_in_dim(window, BAND, rows_here, 0)
    target_cols = lax.dynamic_slice_in_dim(columns, first_slot, share_count, 1)
    target_keep = lax.dynamic_slice_in_dim(keep_mask, first_slot, share_count, 1)
    product = lax.map(one_row, (own_rows, keep_mask, fetch_all, target_cols, target_keep))
    is_first = (fib_index == 0).astype(jnp.float32)
    trace_values = is_first * jnp.sum(
        jnp.diagonal(values[:, 0].astype(jnp.float32), axis1=1, axis2=2)
    )
    trace_square = is_first * jnp.sum(jnp.diagonal(product[:, 0], axis1=1, axis2=2))
    traces = lax.psum(jnp.stack([trace_values, trace_square]), ("row", "col", "fib"))
    return (product.astype(jnp.bfloat16), traces)


LANES = 128
NO_SLOT = 40
TAIL = 16


def vmem():
    return pl.BlockSpec(memory_space=pltpu.VMEM)


def smem():
    return pl.BlockSpec(memory_space=pltpu.SMEM)


def limit(mebibytes):
    return pltpu.CompilerParams(vmem_limit_bytes=mebibytes * 2**20)


LOW_PLACE, HIGH_PLACE = (1, 0, 2, 3), (3, 2, 0, 1)


def turn_into(out_ref, at, blocks, in_ref, half):
    block = in_ref.shape[1]
    width = block // 2
    z = lax.broadcasted_iota(jnp.int32, (width, block), 0) + half * width
    pick = (lax.broadcasted_iota(jnp.int32, (width, block), 1) == z).astype(jnp.bfloat16)
    for n in range(blocks):
        out_ref[at + n * width : at + (n + 1) * width] = lax.dot_general(
            pick, in_ref[n * block : (n + 1) * block], NT, preferred_element_type=jnp.float32
        ).astype(jnp.bfloat16)


def turn_kernel(half_ref, in_ref, out_ref):
    turn_into(out_ref, 0, in_ref.shape[0] // in_ref.shape[1], in_ref, half_ref[0])


def turned_half(half, slab):
    return pl.pallas_call(
        turn_kernel,
        out_shape=jax.ShapeDtypeStruct((slab.shape[0] // 2, slab.shape[1]), slab.dtype),
        in_specs=[smem(), vmem()],
        out_specs=vmem(),
        compiler_params=limit(8),
        name="turn",
    )(half, slab)


def pack_kernel(first_ref, second_ref, out_ref):
    size = out_ref.shape[0] // 2
    out_ref[:size] = first_ref[:size]
    out_ref[size:] = second_ref[:size]


def packed(first, second):
    size = 2 * first.shape[0]
    return pl.pallas_call(
        pack_kernel,
        out_shape=jax.ShapeDtypeStruct((size, first.shape[1]), first.dtype),
        in_specs=[vmem()] * 2,
        out_specs=vmem(),
        compiler_params=limit(8),
        name="pack",
    )(first, second)


def slots_of(group_ref, counts_ref, columns_ref, groups):
    rows, slots = columns_ref.shape
    row = lax.broadcasted_iota(jnp.int32, (rows, slots), 0)
    count = jnp.zeros((rows, slots), jnp.int32)
    for r in range(rows):
        count = jnp.where(row == r, counts_ref[r], count)
    used = lax.broadcasted_iota(jnp.int32, (rows, slots), 1) < count
    total = groups * rows
    distance = columns_ref[...] - (group_ref[0] * rows + row)
    distance = jnp.where(distance > BAND, distance - total, distance)
    distance = jnp.where(distance < -BAND, distance + total, distance)
    return row, used, distance


def find_kernel(groups, group_ref, counts_ref, columns_ref, out_ref):
    rows, slots = columns_ref.shape
    share = slots // 4
    _, used, distance = slots_of(group_ref, counts_ref, columns_ref, groups)
    at = jnp.where(used, distance + 2 * BAND, LANES)
    lane = lax.broadcasted_iota(jnp.int32, (rows, LANES), 1)
    row = lax.broadcasted_iota(jnp.int32, (rows, LANES), 0)
    found = jnp.full((rows, LANES), -1, jnp.int32)
    for s in range(slots):
        p = jnp.where(group_ref[1] == 1, HIGH_PLACE[s // share], LOW_PLACE[s // share])
        found = jnp.where(at[:, s : s + 1] == lane, (p * rows + row) * share + s % share, found)
    out_ref[...] = found


def found_slots(groups, group, columns, counts):
    return pl.pallas_call(
        functools.partial(find_kernel, groups),
        out_shape=jax.ShapeDtypeStruct((columns.shape[0], LANES), jnp.int32),
        in_specs=[smem(), smem(), vmem()],
        out_specs=vmem(),
        compiler_params=limit(2),
        name="find",
    )(group, counts, columns)


def table_kernel(groups, group_ref, counts_ref, columns_ref, own_ref, first_ref, second_ref, out_ref):
    rows, slots = columns_ref.shape
    count = slots // 4 * rows
    nothing = 12 * count
    row, used, distance = slots_of(group_ref, counts_ref, columns_ref, groups)
    out_ref[...] = jnp.full(out_ref.shape, nothing, jnp.int32)
    for n, ref in enumerate((own_ref, first_ref, second_ref)):
        found = ref[...]
        out_ref[n * rows : (n + 1) * rows] = jnp.where(
            found < 0, nothing, found + n * 4 * count
        )
    to = row + distance
    even = group_ref[0] % 2 == 0
    after = jnp.where(even, rows, 2 * rows) - rows
    before = jnp.where(even, 2 * rows, rows) + rows
    to = jnp.where(to >= rows, to + after, jnp.where(to < 0, to + before, to))
    base = to * LANES - distance + 2 * BAND
    base = jnp.where(used, base, 3 * rows * LANES + 2 * BAND)
    out_ref[3 * rows + 1 : 4 * rows + 1, :slots] = base
    out_ref[4 * rows + 1 : 5 * rows + 1, :slots] = jnp.where(used, distance, NO_SLOT)


def slot_table(groups, group, counts, columns, own, first, second):
    height = -(-(5 * columns.shape[0] + 1) // 8) * 8
    table = pl.pallas_call(
        functools.partial(table_kernel, groups),
        out_shape=jax.ShapeDtypeStruct((height, LANES), jnp.int32),
        in_specs=[smem(), smem()] + [vmem()] * 4,
        out_specs=vmem(),
        compiler_params=limit(6),
        name="table",
    )(group, counts, columns, own, first, second)
    return table.reshape(-1)


def collect(right, rights, around, turned):
    size = turned.shape[0]
    for n, ref in enumerate(rights):
        at = (n + n // 3) * size
        right[at : at + size] = ref[:size]
    right[3 * size : 4 * size] = turned[...]
    for m in range(2):
        right[(7 + 4 * m) * size : (8 + 4 * m) * size] = around[m * size : (m + 1) * size]
    rest = right.shape[0] - 12 * size
    right[12 * size :] = jnp.zeros((rest, right.shape[1]), right.dtype)


PARTS = (0, 3, 1, 2)


def product_kernel(sizes, chunk, is_first, table_ref, place_ref, *refs):
    rows, share = sizes
    lefts, rights, around, turned = refs[:4], refs[4:13], refs[13], refs[14]
    outs, right = refs[15:19], refs[19]
    slots = 4 * share
    block = right.shape[1]
    width = block // 2
    base_at = (3 * rows + 1) * LANES
    target_at = base_at + rows * LANES
    collect(right, rights, around, turned)

    def half_at(index):
        return right[pl.ds(pl.multiple_of(index * width, width), width)]

    half, is_low = place_ref[0], place_ref[1] == 1
    start = pl.multiple_of(half * width, width)
    slot_at = [place_ref[2 + a // share] * share + a % share for a in range(slots)]

    def bases_of(r):
        return [table_ref[base_at + r * LANES + slot_at[a]] for a in range(slots)]

    def left_at(a, r, offset, size):
        at = (r * share + a % share) * block
        return lefts[a // share][pl.ds(at + offset, size)]

    for n, r in enumerate(chunk):
        bases = bases_of(r)
        targets = [table_ref[target_at + r * LANES + slot_at[j]] for j in range(slots)]
        product = None
        for a in range(0, slots, 2):
            lines = [
                [half_at(table_ref[bases[a + m] + targets[j]]) for m in range(2)]
                for j in range(slots)
            ]
            stacked = jnp.concatenate([jnp.concatenate(x, axis=1) for x in lines], axis=0)
            left = jnp.concatenate([left_at(a + m, r, 0, block) for m in range(2)], axis=1)
            term = lax.dot_general(stacked, left, NT, preferred_element_type=jnp.float32)
            product = term if product is None else product + term
        for p, out in zip(PARTS, outs):
            for s in range(share):
                j = p * share + s
                out[(n * share + s) * width : (n * share + s + 1) * width] = product[
                    j * width : (j + 1) * width
                ].astype(jnp.bfloat16)
    if not is_first:
        return

    z = lax.broadcasted_iota(jnp.int32, (width, block), 0) + half * width
    on_diagonal = lax.broadcasted_iota(jnp.int32, (width, block), 1) == z
    sum_values = jnp.zeros((width, block), jnp.float32)
    sum_square = jnp.zeros((width, block), jnp.float32)
    for r in range(rows):
        bases = bases_of(r)
        for a in range(slots):
            other = half_at(table_ref[bases[a]])
            mine = left_at(a, r, start, width)
            sum_square += mine.astype(jnp.float32) * other.astype(jnp.float32)
        low, high = (left_at(a, r, start, width).astype(jnp.float32) for a in (share, 3 * share))
        sum_values += jnp.where(on_diagonal, jnp.where(is_low, low, high), 0.0)
    sums = [jnp.sum(s, axis=(0, 1), keepdims=True) for s in (sum_values, sum_square)]
    lane = lax.broadcasted_iota(jnp.int32, (TAIL, block), 1)
    tail = jnp.zeros((TAIL, block), jnp.float32)
    for n, rest in enumerate(sums):
        for m in range(3):
            term = rest.astype(jnp.bfloat16).astype(jnp.float32)
            tail = jnp.where(lane == 2 * m + n, term, tail)
            rest = rest - term
    for out in outs:
        out[len(chunk) * share * width :] = tail.astype(jnp.bfloat16)


def products(sizes, chunk, is_first, table, place, lefts, *rest):
    rows, share = sizes
    block = lefts[0].shape[1]
    width, slots = block // 2, 4 * share
    length = len(chunk) * share * width + (TAIL if is_first else 0)
    shapes = [(length, block)] * 4
    operands = [*lefts, *rest]
    flops = 2 * len(chunk) * slots * slots * width * block * block
    return pl.pallas_call(
        functools.partial(product_kernel, sizes, chunk, is_first),
        out_shape=[jax.ShapeDtypeStruct(shape, jnp.bfloat16) for shape in shapes],
        in_specs=[smem(), smem()] + [vmem()] * len(operands),
        out_specs=[vmem()] * len(shapes),
        scratch_shapes=[pltpu.VMEM(((12 * rows * share + 1) * width, block), jnp.bfloat16)],
        compiler_params=limit(32),
        cost_estimate=pl.CostEstimate(flops=flops, bytes_accessed=4 * 2**20, transcendentals=0),
        name="products",
    )(table, place, *operands)


PLANE_PARTS = ((2, 1), (0, 3), (3, 0), (1, 2))


def add_kernel(fib_ref, own_ref, far_ref, near_ref, mid_ref, out_ref):
    parts = (own_ref, far_ref, near_ref, mid_ref)

    def write(*pair):
        first, second = (p[p.shape[0] - TAIL :].astype(jnp.float32) for p in pair)
        lane = lax.broadcasted_iota(jnp.int32, first.shape, 1)
        totals = []
        for n in range(2):
            terms = [
                [
                    jnp.sum(jnp.where(lane == 2 * m + n, p, 0.0), axis=1, keepdims=True)
                    for m in range(3)
                ]
                for p in (first, second)
            ]
            a, b = (t[0] + (t[1] + t[2]) for t in terms)
            totals.append(a + b)
        total = jnp.where(lane == 0, totals[0], jnp.where(lane == 1, totals[1], 0.0))
        out_ref[...] = total[:8]

    for plane, pair in enumerate(PLANE_PARTS):
        pl.when(fib_ref[0] == plane)(functools.partial(write, *(parts[n] for n in pair)))


def added(fib, parts):
    return pl.pallas_call(
        add_kernel,
        out_shape=jax.ShapeDtypeStruct((8, 128), jnp.float32),
        in_specs=[smem()] + [vmem()] * 4,
        out_specs=vmem(),
        compiler_params=limit(6),
        name="add",
    )(fib, *parts)


def join_kernel(chunks, fib_ref, *refs):
    out_ref = refs[-1]
    share, block = out_ref.shape[1:3]
    width = block // 2

    def write(*pair):
        for c, chunk in enumerate(chunks):
            for n, r in enumerate(chunk):
                for s in range(share):
                    at = (n * share + s) * width
                    halves = [refs[4 * c + p][at : at + width] for p in pair]
                    out_ref[r, s] = jnp.concatenate(halves, axis=0).T

    for plane, pair in enumerate(PLANE_PARTS):
        pl.when(fib_ref[0] == plane)(functools.partial(write, *pair))


def joined(sizes, chunks, fib, parts):
    block = parts[0].shape[1]
    return pl.pallas_call(
        functools.partial(join_kernel, chunks),
        out_shape=jax.ShapeDtypeStruct((*sizes, block, block), parts[0].dtype),
        in_specs=[smem()] + [vmem()] * len(parts),
        out_specs=vmem(),
        compiler_params=limit(8),
        name="join",
    )(fib, *parts)


def middle_body(groups, values, columns, counts):
    rows, share, block, _ = values.shape
    fib = lax.axis_index("fib")
    group = lax.axis_index(PLANE)
    high = fib >= 2

    low_order, high_order = (1, 0, 2, 3), (2, 3, 1, 0)
    inward = [[(0, 1), (3, 2)], [(1, 2), (2, 1)], [(0, 2), (3, 1)]]
    outward = [[(j, i) for i, j in pairs] for pairs in inward]

    def middle(pairs):
        return [(i * 4 + f, j * 4 + f) for i, j in pairs for f in (1, 2)]

    swap = [(i, i ^ 1) for i in range(groups)]
    skip = [((i + 2) % groups if i % 2 else (i - 2) % groups, i) for i in range(groups)]

    def from_both_middle(array, *before):
        first = lax.ppermute(array, ALL, middle(swap))
        passed, *_ = lax.optimization_barrier((first, *before))
        return first, lax.ppermute(passed, ALL, middle(skip))

    flat = values.reshape(rows * share * block, block)
    near, mid = (lax.ppermute(flat, "fib", pairs) for pairs in inward[:2])

    half = jnp.where(high, 1, 0).astype(jnp.int32)
    own_half = (1 - fib % 2).astype(jnp.int32)
    own = turned_half(own_half.reshape(1), flat)
    own_first = lax.ppermute(own, PLANE, swap)
    group_ref = jnp.stack([group, half]).astype(jnp.int32)
    found = found_slots(groups, group_ref, columns, counts)
    found_first = lax.ppermute(found, PLANE, swap)
    own_passed, _ = lax.optimization_barrier((own_first, found_first))
    own_second = lax.ppermute(own_passed, PLANE, skip)
    later, *_ = lax.optimization_barrier((flat, own_first))
    far = lax.ppermute(later, "fib", inward[2])
    near_turned, mid_turned, far_turned = (
        turned_half(half.reshape(1), slab) for slab in (near, mid, far)
    )
    found_second = lax.ppermute(found_first, PLANE, skip)
    first, second, *_ = lax.optimization_barrier((own_first, own_second, found_second))
    far_around = lax.ppermute(packed(first, second), "fib", inward[2])
    table = slot_table(groups, group_ref, counts, columns, found, found_first, found_second)
    near_around = from_both_middle(near_turned)
    mid_around = from_both_middle(mid_turned)
    rights = [own, near_turned, mid_turned]
    rights += [own_first, near_around[0], mid_around[0]]
    rights += [own_second, near_around[1], mid_around[1]]

    place = [half, 1 - half]
    place += [jnp.where(high, h, l) for l, h in zip(low_order, high_order)]
    place = jnp.stack(place).astype(jnp.int32)
    sizes = (rows, share)
    chunks = (range(rows // 2), range(rows // 2, rows))
    gathered = []
    lefts, rest = [flat, near, mid, far], [*rights, far_around, far_turned]
    for n, chunk in enumerate(chunks):
        own_part, *parts = products(sizes, chunk, n == 0, table, place, lefts, *rest)
        gathered.append(own_part)
        gathered += [
            lax.ppermute(part, "fib", outward[m - 1]) for m, part in zip(PARTS[1:], parts)
        ]
    fib_ref = fib.reshape(1).astype(jnp.int32)
    sums = added(fib_ref, gathered[:4])
    square = joined(sizes, chunks, fib_ref, gathered)

    def moved(array, bits):
        return lax.ppermute(array, PLANE, [(i, i ^ bits) for i in range(groups)])

    bits = [1 << n for n in range(groups.bit_length() - 1)]
    if len(bits) % 2:
        alone = bits.pop(len(bits) // 2)
        sums = sums + moved(sums, alone)
    while bits:
        one, two = bits.pop(0), bits.pop()
        a, b, c = moved(sums, one), moved(sums, two), moved(sums, one | two)
        sums = (sums + a) + (b + c)
    return square, sums[0, :2]


def solution(mesh):
    in_specs = (P(("row", "col"), "fib", None, None), P(("row", "col"), None), P(("row", "col")))
    out_specs = (P(("row", "col"), "fib", None, None), P())
    groups = mesh.shape["row"] * mesh.shape["col"]

    def body(values, columns, counts):
        rows, share = values.shape[:2]
        fits = groups >= 4 and groups & (groups - 1) == 0 and mesh.shape["fib"] == 4
        if fits and BAND <= rows <= TAIL and rows * share <= 64:
            return middle_body(groups, values, columns, counts)
        return general_body(values, columns, counts)

    return jax.shard_map(body, mesh=mesh, in_specs=in_specs, out_specs=out_specs, check_vma=False)
```

profile of v0, /device:TPU:0, one launch (start us, length us, event | category | flops | bytes accessed | tf_op | source)
XLA Modules:
  0.0 73.4 jit_solution(1154771281651283746)
XLA Ops:
  0.6 5.0 %collective-permute-start.2 = (bf16[2304,128]{1,0:T(8,128)(2,1)}, bf16[2304,128]{1,0:T(8,128)(2,1)S(1)}, u32[]{:S(2)}, u32[]{:S(2)}) collective-permute-start(bf16[2304,128]{1,0:T(8,128)(2,1)} %bitcast.13), channel_id=1, source_target_pairs={{0,1},{3,2},{4,5},{7,6},{8,9},{11,10},{12,13},{15,14},{16,17},{19,... | collective-permute-start | bytes 1769480 | tf_op jit(solution)/shard_map/ppermute | solution.py:412
  5.6 0.7 collective-permute-start.3
  6.3 1.1 %copy-done = bf16[6,3,128,128]{3,2,1,0:T(8,128)(2,1)S(1)} copy-done((bf16[6,3,128,128]{3,2,1,0:T(8,128)(2,1)S(1)}, bf16[6,3,128,128]{3,2,1,0:T(8,128)(2,1)}, u32[]{:S(2)}) %copy-start) | copy-done | bytes 589848
  7.9 1.5 %collective-permute-start.4 = (bf16[1152,128]{1,0:T(8,128)(2,1)S(1)}, bf16[1152,128]{1,0:T(8,128)(2,1)S(1)}, u32[]{:S(2)}, u32[]{:S(2)}) collective-permute-start(bf16[1152,128]{1,0:T(8,128)(2,1)S(1)} %turn.4.refs_4_), channel_id=1, source_target_pairs={{0,4},{4,0},{8,12},{12,8},{16,20},{20,16},{24,28},{28,24},{1,5},{5... | collective-permute-start | bytes 884744 | tf_op jit(solution)/shard_map/ppermute | solution.py:417
  10.1 0.6 find.1.own_ref
  11.4 5.1 %collective-permute-done.first_ref = s32[6,128]{1,0:T(8,128)S(1)} collective-permute-done((s32[6,128]{1,0:T(8,128)S(1)}, s32[6,128]{1,0:T(8,128)S(1)}, u32[]{:S(2)}, u32[]{:S(2)}) %collective-permute-start) | collective-permute-done | bytes 3104 | tf_op jit(solution)/shard_map/ppermute | solution.py:420
  16.5 1.6 %collective-permute-start.1 = (s32[6,128]{1,0:T(8,128)S(1)}, s32[6,128]{1,0:T(8,128)S(1)}, u32[]{:S(2)}, u32[]{:S(2)}) collective-permute-start(s32[6,128]{1,0:T(8,128)S(1)} %collective-permute-done.first_ref), channel_id=1, source_target_pairs={{24,0},{12,4},{0,8},{20,12},{8,16},{28,20},{16,24},{4,28},{25,1},{... | collective-permute-start | bytes 9224 | tf_op jit(solution)/shard_map/ppermute | solution.py:428
  18.1 4.0 %collective-permute-start.5 = (bf16[2304,128]{1,0:T(8,128)(2,1)S(1)}, bf16[2304,128]{1,0:T(8,128)(2,1)S(1)}, u32[]{:S(2)}, u32[]{:S(2)}) collective-permute-start(bf16[2304,128]{1,0:T(8,128)(2,1)S(1)} %bitcast.16), channel_id=1, source_target_pairs={{0,2},{3,1},{4,6},{7,5},{8,10},{11,9},{12,14},{15,13},{16,18},{19,... | collective-permute-start | bytes 1769480 | tf_op jit(solution)/shard_map/ppermute | solution.py:424
  22.6 1.4 %collective-permute-start.6 = (bf16[1152,128]{1,0:T(8,128)(2,1)S(1)}, bf16[1152,128]{1,0:T(8,128)(2,1)}, u32[]{:S(2)}, u32[]{:S(2)}) collective-permute-start(bf16[1152,128]{1,0:T(8,128)(2,1)S(1)} %turn.5.refs_5_), channel_id=1, source_target_pairs={{1,5},{2,6},{5,1},{6,2},{9,13},{10,14},{13,9},{14,10},{17,21},{18,... | collective-permute-start | bytes 884744 | tf_op jit(solution)/shard_map/ppermute | solution.py:407
  24.5 1.4 %collective-permute-start.7 = (bf16[1152,128]{1,0:T(8,128)(2,1)S(1)}, bf16[1152,128]{1,0:T(8,128)(2,1)}, u32[]{:S(2)}, u32[]{:S(2)}) collective-permute-start(bf16[1152,128]{1,0:T(8,128)(2,1)S(1)} %turn.6.refs_6_), channel_id=1, source_target_pairs={{1,5},{2,6},{5,1},{6,2},{9,13},{10,14},{13,9},{14,10},{17,21},{18,... | collective-permute-start | bytes 884744 | tf_op jit(solution)/shard_map/ppermute | solution.py:407
  25.9 0.9 %pack.1 = bf16[2304,128]{1,0:T(8,128)(2,1)} custom-call(bf16[1152,128]{1,0:T(8,128)(2,1)S(1)} %collective-permute-done.4.first_ref.refs_7_, bf16[1152,128]{1,0:T(8,128)(2,1)S(1)} %collective-permute-done.8.second_ref.refs_10_), custom_call_target="tpu_custom_call" | custom-call | tf_op jit(solution)/shard_map/pack/pallas_call | solution.py:133
  26.9 5.5 %collective-permute-start.11 = (bf16[2304,128]{1,0:T(8,128)(2,1)}, bf16[2304,128]{1,0:T(8,128)(2,1)}, u32[]{:S(2)}, u32[]{:S(2)}) collective-permute-start(bf16[2304,128]{1,0:T(8,128)(2,1)} %pack.1), channel_id=1, source_target_pairs={{0,2},{3,1},{4,6},{7,5},{8,10},{11,9},{12,14},{15,13},{16,18},{19,... | collective-permute-start | bytes 1769480 | tf_op jit(solution)/shard_map/ppermute | solution.py:430
  32.4 1.4 %collective-permute-start.9 = (bf16[1152,128]{1,0:T(8,128)(2,1)}, bf16[1152,128]{1,0:T(8,128)(2,1)}, u32[]{:S(2)}, u32[]{:S(2)}) collective-permute-start(bf16[1152,128]{1,0:T(8,128)(2,1)} %collective-permute-done.6.refs_8_), channel_id=1, source_target_pairs={{25,1},{26,2},{13,5},{14,6},{1,9},{2,10},{21,13},{22,14},{9,17},{1... | collective-permute-start | bytes 884744 | tf_op jit(solution)/shard_map/ppermute | solution.py:409
  33.8 1.4 %collective-permute-start.10 = (bf16[1152,128]{1,0:T(8,128)(2,1)}, bf16[1152,128]{1,0:T(8,128)(2,1)}, u32[]{:S(2)}, u32[]{:S(2)}) collective-permute-start(bf16[1152,128]{1,0:T(8,128)(2,1)} %collective-permute-done.7.refs_9_), channel_id=1, source_target_pairs={{25,1},{26,2},{13,5},{14,6},{1,9},{2,10},{21,13},{22,14},{9,17},{1... | collective-permute-start | bytes 884744 | tf_op jit(solution)/shard_map/ppermute | solution.py:409
  35.2 0.7 copy-done.6
  35.9 0.7 copy-done.8
  36.6 0.7 copy-done.10
  38.3 9.3 %collective-permute-done.11.refs_13_ = bf16[2304,128]{1,0:T(8,128)(2,1)} collective-permute-done((bf16[2304,128]{1,0:T(8,128)(2,1)}, bf16[2304,128]{1,0:T(8,128)(2,1)}, u32[]{:S(2)}, u32[]{:S(2)}) %collective-permute-start.11) | collective-permute-done | bytes 589856 | tf_op jit(solution)/shard_map/ppermute | solution.py:430
  47.6 3.7 %products.2 = (bf16[592,128]{1,0:T(8,128)(2,1)S(1)}, bf16[592,128]{1,0:T(8,128)(2,1)S(1)}, bf16[592,128]{1,0:T(8,128)(2,1)S(1)}, bf16[592,128]{1,0:T(8,128)(2,1)S(1)}) custom-call(s32[4096]{0:T(1024)S(1)} %bitcast.19, s32[6]{0:T(128)S(1)} %stack.36.place_ref, bf16[2304,128]{1,0:T(8,128)(2,1)S(1)} %bitcast.17, ...), custom_call_target="tpu_custom_call" | custom-call | flops 905969664 | bytes 4194304 | tf_op jit(solution)/shard_map/products/pallas_call | solution.py:311
  51.3 1.3 %collective-permute-start.12 = (bf16[592,128]{1,0:T(8,128)(2,1)S(1)}, bf16[592,128]{1,0:T(8,128)(2,1)S(1)}, u32[]{:S(2)}, u32[]{:S(2)}) collective-permute-start(bf16[592,128]{1,0:T(8,128)(2,1)S(1)} %get-tuple-element.19), channel_id=1, source_target_pairs={{2,0},{1,3},{6,4},{5,7},{10,8},{9,11},{14,12},{13,15},{18,16},{17,... | collective-permute-start | bytes 454664 | tf_op jit(solution)/shard_map/ppermute | solution.py:449
  52.6 1.3 %collective-permute-start.13 = (bf16[592,128]{1,0:T(8,128)(2,1)S(1)}, bf16[592,128]{1,0:T(8,128)(2,1)S(1)}, u32[]{:S(2)}, u32[]{:S(2)}) collective-permute-start(bf16[592,128]{1,0:T(8,128)(2,1)S(1)} %get-tuple-element.20), channel_id=1, source_target_pairs={{1,0},{2,3},{5,4},{6,7},{9,8},{10,11},{13,12},{14,15},{17,16},{18,... | collective-permute-start | bytes 454664 | tf_op jit(solution)/shard_map/ppermute | solution.py:449
  53.9 0.7 collective-permute-start.14
  54.6 3.6 %products.3 = (bf16[576,128]{1,0:T(8,128)(2,1)S(1)}, bf16[576,128]{1,0:T(8,128)(2,1)S(1)}, bf16[576,128]{1,0:T(8,128)(2,1)S(1)}, bf16[576,128]{1,0:T(8,128)(2,1)S(1)}) custom-call(s32[4096]{0:T(1024)S(1)} %bitcast.20, s32[6]{0:T(128)S(1)} %stack.36.place_ref, bf16[2304,128]{1,0:T(8,128)(2,1)S(1)} %bitcast.18, ...), custom_call_target="tpu_custom_call" | custom-call | flops 905969664 | bytes 4194304 | tf_op jit(solution)/shard_map/products/pallas_call | solution.py:311
  58.3 1.3 %collective-permute-start.15 = (bf16[576,128]{1,0:T(8,128)(2,1)S(1)}, bf16[576,128]{1,0:T(8,128)(2,1)S(1)}, u32[]{:S(2)}, u32[]{:S(2)}) collective-permute-start(bf16[576,128]{1,0:T(8,128)(2,1)S(1)} %get-tuple-element.23), channel_id=1, source_target_pairs={{2,0},{1,3},{6,4},{5,7},{10,8},{9,11},{14,12},{13,15},{18,16},{17,... | collective-permute-start | bytes 442376 | tf_op jit(solution)/shard_map/ppermute | solution.py:449
  59.6 1.3 %collective-permute-start.16 = (bf16[576,128]{1,0:T(8,128)(2,1)S(1)}, bf16[576,128]{1,0:T(8,128)(2,1)S(1)}, u32[]{:S(2)}, u32[]{:S(2)}) collective-permute-start(bf16[576,128]{1,0:T(8,128)(2,1)S(1)} %get-tuple-element.24), channel_id=1, source_target_pairs={{1,0},{2,3},{5,4},{6,7},{9,8},{10,11},{13,12},{14,15},{17,16},{18,... | collective-permute-start | bytes 442376 | tf_op jit(solution)/shard_map/ppermute | solution.py:449
  60.9 0.7 collective-permute-start.17
  61.5 1.0 %collective-permute-done.13.refs_2_.near_ref = bf16[592,128]{1,0:T(8,128)(2,1)S(1)} collective-permute-done((bf16[592,128]{1,0:T(8,128)(2,1)S(1)}, bf16[592,128]{1,0:T(8,128)(2,1)S(1)}, u32[]{:S(2)}, u32[]{:S(2)}) %collective-permute-start.13) | collective-permute-done | bytes 151584 | tf_op jit(solution)/shard_map/ppermute | solution.py:449
  62.7 1.1 %collective-permute-done.18 = f32[8,128]{1,0:T(8,128)S(1)} collective-permute-done((f32[8,128]{1,0:T(8,128)S(1)}, f32[8,128]{1,0:T(8,128)S(1)}, u32[]{:S(2)}, u32[]{:S(2)}) %collective-permute-start.18) | collective-permute-done | bytes 4128 | tf_op jit(solution)/shard_map/ppermute | solution.py:456
  65.0 4.1 %collective-permute-done.15.refs_5_ = bf16[576,128]{1,0:T(8,128)(2,1)S(1)} collective-permute-done((bf16[576,128]{1,0:T(8,128)(2,1)S(1)}, bf16[576,128]{1,0:T(8,128)(2,1)S(1)}, u32[]{:S(2)}, u32[]{:S(2)}) %collective-permute-start.15) | collective-permute-done | bytes 147488 | tf_op jit(solution)/shard_map/ppermute | solution.py:449
  69.1 1.6 %collective-permute-start.19 = (f32[8,128]{1,0:T(8,128)S(1)}, f32[8,128]{1,0:T(8,128)S(1)}, u32[]{:S(2)}, u32[]{:S(2)}) collective-permute-start(f32[8,128]{1,0:T(8,128)S(1)} %add.22), channel_id=1, source_target_pairs={{0,4},{4,0},{8,12},{12,8},{16,20},{20,16},{24,28},{28,24},{1,5},{5... | collective-permute-start | bytes 12296 | tf_op jit(solution)/shard_map/ppermute | solution.py:456
  70.7 1.1 %collective-permute-done.16.refs_6_ = bf16[576,128]{1,0:T(8,128)(2,1)S(1)} collective-permute-done((bf16[576,128]{1,0:T(8,128)(2,1)S(1)}, bf16[576,128]{1,0:T(8,128)(2,1)S(1)}, u32[]{:S(2)}, u32[]{:S(2)}) %collective-permute-start.16) | collective-permute-done | bytes 147488 | tf_op jit(solution)/shard_map/ppermute | solution.py:449
  71.8 1.0 %join.1 = bf16[6,3,128,128]{3,2,1,0:T(8,128)(2,1)} custom-call(s32[1]{0:T(128)} %bitcast.fib_ref, bf16[592,128]{1,0:T(8,128)(2,1)S(1)} %get-tuple-element.18.refs_0_.own_ref, bf16[592,128]{1,0:T(8,128)(2,1)S(1)} %collective-permute-done.12.refs_1_.far_ref, bf16[592,128]{1,0:T(8,128)(2,1)S(1)} %collective-permute-done.13.refs_2_.near_ref, ...), custom_call_target="tpu_custom_call" | custom-call | tf_op jit(solution)/shard_map/join/pallas_call | solution.py:380
  (50 shorter events, 5.8 us)
Async XLA Ops:
  0.6 21.5 %collective-permute-start.2 = (bf16[2304,128]{1,0:T(8,128)(2,1)}, bf16[2304,128]{1,0:T(8,128)(2,1)S(1)}, u32[]{:S(2)}, u32[]{:S(2)}) collective-permute-start(bf16[2304,128]{1,0:T(8,128)(2,1)} %bitcast.13), channel_id=1, source_target_pairs={{0,1},{3,2},{4,5},{7,6},{8,9},{11,10},{12,13},{15,14},{16,17},{19,... | collective-permute-start | bytes 1769480 | tf_op jit(solution)/shard_map/ppermute | solution.py:412
  5.6 18.4 %collective-permute-start.3 = (bf16[2304,128]{1,0:T(8,128)(2,1)}, bf16[2304,128]{1,0:T(8,128)(2,1)S(1)}, u32[]{:S(2)}, u32[]{:S(2)}) collective-permute-start(bf16[2304,128]{1,0:T(8,128)(2,1)} %bitcast.14), channel_id=1, source_target_pairs={{1,2},{2,1},{5,6},{6,5},{9,10},{10,9},{13,14},{14,13},{17,18},{18,... | collective-permute-start | bytes 1769480 | tf_op jit(solution)/shard_map/ppermute | solution.py:412
  6.3 1.1 %copy-start = (bf16[6,3,128,128]{3,2,1,0:T(8,128)(2,1)S(1)}, bf16[6,3,128,128]{3,2,1,0:T(8,128)(2,1)}, u32[]{:S(2)}) copy-start(bf16[6,3,128,128]{3,2,1,0:T(8,128)(2,1)} %param.3) | copy-start | bytes 1769476
  7.4 10.8 %copy-start.1 = (bf16[6,3,128,128]{3,2,1,0:T(8,128)(2,1)S(1)}, bf16[6,3,128,128]{3,2,1,0:T(8,128)(2,1)}, u32[]{:S(2)}) copy-start(bf16[6,3,128,128]{3,2,1,0:T(8,128)(2,1)} %param.3) | copy-start | bytes 1769476
  7.9 8.6 %collective-permute-start.4 = (bf16[1152,128]{1,0:T(8,128)(2,1)S(1)}, bf16[1152,128]{1,0:T(8,128)(2,1)S(1)}, u32[]{:S(2)}, u32[]{:S(2)}) collective-permute-start(bf16[1152,128]{1,0:T(8,128)(2,1)S(1)} %turn.4.refs_4_), channel_id=1, source_target_pairs={{0,4},{4,0},{8,12},{12,8},{16,20},{20,16},{24,28},{28,24},{1,5},{5... | collective-permute-start | bytes 884744 | tf_op jit(solution)/shard_map/ppermute | solution.py:417
  9.4 0.7 copy-start.4
  9.4 0.7 copy-start.7
  10.8 5.7 %collective-permute-start = (s32[6,128]{1,0:T(8,128)S(1)}, s32[6,128]{1,0:T(8,128)S(1)}, u32[]{:S(2)}, u32[]{:S(2)}) collective-permute-start(s32[6,128]{1,0:T(8,128)S(1)} %find.1.own_ref), channel_id=1, source_target_pairs={{0,4},{4,0},{8,12},{12,8},{16,20},{20,16},{24,28},{28,24},{1,5},{5... | collective-permute-start | bytes 9224 | tf_op jit(solution)/shard_map/ppermute | solution.py:420
  16.5 9.4 %collective-permute-start.8 = (bf16[1152,128]{1,0:T(8,128)(2,1)S(1)}, bf16[1152,128]{1,0:T(8,128)(2,1)S(1)}, u32[]{:S(2)}, u32[]{:S(2)}) collective-permute-start(bf16[1152,128]{1,0:T(8,128)(2,1)S(1)} %collective-permute-done.4.first_ref.refs_7_), channel_id=1, source_target_pairs={{24,0},{12,4},{0,8},{20,12},{8,16},{28,20},{16,24},{4,28},{25,1},{... | collective-permute-start | bytes 884744 | tf_op jit(solution)/shard_map/ppermute | solution.py:422
  16.5 9.4 %collective-permute-start.1 = (s32[6,128]{1,0:T(8,128)S(1)}, s32[6,128]{1,0:T(8,128)S(1)}, u32[]{:S(2)}, u32[]{:S(2)}) collective-permute-start(s32[6,128]{1,0:T(8,128)S(1)} %collective-permute-done.first_ref), channel_id=1, source_target_pairs={{24,0},{12,4},{0,8},{20,12},{8,16},{28,20},{16,24},{4,28},{25,1},{... | collective-permute-start | bytes 9224 | tf_op jit(solution)/shard_map/ppermute | solution.py:428
  18.1 19.7 %collective-permute-start.5 = (bf16[2304,128]{1,0:T(8,128)(2,1)S(1)}, bf16[2304,128]{1,0:T(8,128)(2,1)S(1)}, u32[]{:S(2)}, u32[]{:S(2)}) collective-permute-start(bf16[2304,128]{1,0:T(8,128)(2,1)S(1)} %bitcast.16), channel_id=1, source_target_pairs={{0,2},{3,1},{4,6},{7,5},{8,10},{11,9},{12,14},{15,13},{16,18},{19,... | collective-permute-start | bytes 1769480 | tf_op jit(solution)/shard_map/ppermute | solution.py:424
  22.6 9.7 %collective-permute-start.6 = (bf16[1152,128]{1,0:T(8,128)(2,1)S(1)}, bf16[1152,128]{1,0:T(8,128)(2,1)}, u32[]{:S(2)}, u32[]{:S(2)}) collective-permute-start(bf16[1152,128]{1,0:T(8,128)(2,1)S(1)} %turn.5.refs_5_), channel_id=1, source_target_pairs={{1,5},{2,6},{5,1},{6,2},{9,13},{10,14},{13,9},{14,10},{17,21},{18,... | collective-permute-start | bytes 884744 | tf_op jit(solution)/shard_map/ppermute | solution.py:407
  24.5 9.2 %collective-permute-start.7 = (bf16[1152,128]{1,0:T(8,128)(2,1)S(1)}, bf16[1152,128]{1,0:T(8,128)(2,1)}, u32[]{:S(2)}, u32[]{:S(2)}) collective-permute-start(bf16[1152,128]{1,0:T(8,128)(2,1)S(1)} %turn.6.refs_6_), channel_id=1, source_target_pairs={{1,5},{2,6},{5,1},{6,2},{9,13},{10,14},{13,9},{14,10},{17,21},{18,... | collective-permute-start | bytes 884744 | tf_op jit(solution)/shard_map/ppermute | solution.py:407
  25.9 0.9 %copy-start.5 = (s32[6,128]{1,0:T(8,128)}, s32[6,128]{1,0:T(8,128)S(1)}, u32[]{:S(2)}) copy-start(s32[6,128]{1,0:T(8,128)S(1)} %collective-permute-done.1.second_ref) | copy-start | bytes 9220
  25.9 0.9 %copy-start.2 = (bf16[1152,128]{1,0:T(8,128)(2,1)}, bf16[1152,128]{1,0:T(8,128)(2,1)S(1)}, u32[]{:S(2)}) copy-start(bf16[1152,128]{1,0:T(8,128)(2,1)S(1)} %collective-permute-done.8.second_ref.refs_10_) | copy-start | bytes 884740
  26.9 20.8 %collective-permute-start.11 = (bf16[2304,128]{1,0:T(8,128)(2,1)}, bf16[2304,128]{1,0:T(8,128)(2,1)}, u32[]{:S(2)}, u32[]{:S(2)}) collective-permute-start(bf16[2304,128]{1,0:T(8,128)(2,1)} %pack.1), channel_id=1, source_target_pairs={{0,2},{3,1},{4,6},{7,5},{8,10},{11,9},{12,14},{15,13},{16,18},{19,... | collective-permute-start | bytes 1769480 | tf_op jit(solution)/shard_map/ppermute | solution.py:430
  32.4 6.0 %collective-permute-start.9 = (bf16[1152,128]{1,0:T(8,128)(2,1)}, bf16[1152,128]{1,0:T(8,128)(2,1)}, u32[]{:S(2)}, u32[]{:S(2)}) collective-permute-start(bf16[1152,128]{1,0:T(8,128)(2,1)} %collective-permute-done.6.refs_8_), channel_id=1, source_target_pairs={{25,1},{26,2},{13,5},{14,6},{1,9},{2,10},{21,13},{22,14},{9,17},{1... | collective-permute-start | bytes 884744 | tf_op jit(solution)/shard_map/ppermute | solution.py:409
  33.8 4.6 %collective-permute-start.10 = (bf16[1152,128]{1,0:T(8,128)(2,1)}, bf16[1152,128]{1,0:T(8,128)(2,1)}, u32[]{:S(2)}, u32[]{:S(2)}) collective-permute-start(bf16[1152,128]{1,0:T(8,128)(2,1)} %collective-permute-done.7.refs_9_), channel_id=1, source_target_pairs={{25,1},{26,2},{13,5},{14,6},{1,9},{2,10},{21,13},{22,14},{9,17},{1... | collective-permute-start | bytes 884744 | tf_op jit(solution)/shard_map/ppermute | solution.py:409
  35.2 0.7 copy-start.6
  35.9 0.7 copy-start.8
  36.6 0.7 copy-start.10
  37.8 9.8 %copy-start.3 = (bf16[1152,128]{1,0:T(8,128)(2,1)S(1)}, bf16[1152,128]{1,0:T(8,128)(2,1)}, u32[]{:S(2)}) copy-start(bf16[1152,128]{1,0:T(8,128)(2,1)} %copy-done.2) | copy-start | bytes 884740
  51.3 9.5 %collective-permute-start.12 = (bf16[592,128]{1,0:T(8,128)(2,1)S(1)}, bf16[592,128]{1,0:T(8,128)(2,1)S(1)}, u32[]{:S(2)}, u32[]{:S(2)}) collective-permute-start(bf16[592,128]{1,0:T(8,128)(2,1)S(1)} %get-tuple-element.19), channel_id=1, source_target_pairs={{2,0},{1,3},{6,4},{5,7},{10,8},{9,11},{14,12},{13,15},{18,16},{17,... | collective-permute-start | bytes 454664 | tf_op jit(solution)/shard_map/ppermute | solution.py:449
  52.6 9.9 %collective-permute-start.13 = (bf16[592,128]{1,0:T(8,128)(2,1)S(1)}, bf16[592,128]{1,0:T(8,128)(2,1)S(1)}, u32[]{:S(2)}, u32[]{:S(2)}) collective-permute-start(bf16[592,128]{1,0:T(8,128)(2,1)S(1)} %get-tuple-element.20), channel_id=1, source_target_pairs={{1,0},{2,3},{5,4},{6,7},{9,8},{10,11},{13,12},{14,15},{17,16},{18,... | collective-permute-start | bytes 454664 | tf_op jit(solution)/shard_map/ppermute | solution.py:449
  53.9 8.6 %collective-permute-start.14 = (bf16[592,128]{1,0:T(8,128)(2,1)S(1)}, bf16[592,128]{1,0:T(8,128)(2,1)S(1)}, u32[]{:S(2)}, u32[]{:S(2)}) collective-permute-start(bf16[592,128]{1,0:T(8,128)(2,1)S(1)} %get-tuple-element.21), channel_id=1, source_target_pairs={{2,1},{1,2},{6,5},{5,6},{10,9},{9,10},{14,13},{13,14},{18,17},{17,... | collective-permute-start | bytes 454664 | tf_op jit(solution)/shard_map/ppermute | solution.py:449
  58.3 10.8 %collective-permute-start.15 = (bf16[576,128]{1,0:T(8,128)(2,1)S(1)}, bf16[576,128]{1,0:T(8,128)(2,1)S(1)}, u32[]{:S(2)}, u32[]{:S(2)}) collective-permute-start(bf16[576,128]{1,0:T(8,128)(2,1)S(1)} %get-tuple-element.23), channel_id=1, source_target_pairs={{2,0},{1,3},{6,4},{5,7},{10,8},{9,11},{14,12},{13,15},{18,16},{17,... | collective-permute-start | bytes 442376 | tf_op jit(solution)/shard_map/ppermute | solution.py:449
  59.6 12.3 %collective-permute-start.16 = (bf16[576,128]{1,0:T(8,128)(2,1)S(1)}, bf16[576,128]{1,0:T(8,128)(2,1)S(1)}, u32[]{:S(2)}, u32[]{:S(2)}) collective-permute-start(bf16[576,128]{1,0:T(8,128)(2,1)S(1)} %get-tuple-element.24), channel_id=1, source_target_pairs={{1,0},{2,3},{5,4},{6,7},{9,8},{10,11},{13,12},{14,15},{17,16},{18,... | collective-permute-start | bytes 442376 | tf_op jit(solution)/shard_map/ppermute | solution.py:449
  60.9 11.0 %collective-permute-start.17 = (bf16[576,128]{1,0:T(8,128)(2,1)S(1)}, bf16[576,128]{1,0:T(8,128)(2,1)S(1)}, u32[]{:S(2)}, u32[]{:S(2)}) collective-permute-start(bf16[576,128]{1,0:T(8,128)(2,1)S(1)} %get-tuple-element.25), channel_id=1, source_target_pairs={{2,1},{1,2},{6,5},{5,6},{10,9},{9,10},{14,13},{13,14},{18,17},{17,... | collective-permute-start | bytes 442376 | tf_op jit(solution)/shard_map/ppermute | solution.py:449
  62.6 1.2 %collective-permute-start.18 = (f32[8,128]{1,0:T(8,128)S(1)}, f32[8,128]{1,0:T(8,128)S(1)}, u32[]{:S(2)}, u32[]{:S(2)}) collective-permute-start(f32[8,128]{1,0:T(8,128)S(1)} %add.31), channel_id=1, source_target_pairs={{0,8},{4,12},{8,0},{12,4},{16,24},{20,28},{24,16},{28,20},{1,9},{5... | collective-permute-start | bytes 12296 | tf_op jit(solution)/shard_map/ppermute | solution.py:456
  63.8 9.1 %collective-permute-start.20 = (f32[8,128]{1,0:T(8,128)S(1)}, f32[8,128]{1,0:T(8,128)S(1)}, u32[]{:S(2)}, u32[]{:S(2)}) collective-permute-start(f32[8,128]{1,0:T(8,128)S(1)} %add.22), channel_id=1, source_target_pairs={{0,16},{4,20},{8,24},{12,28},{16,0},{20,4},{24,8},{28,12},{1,17},{... | collective-permute-start | bytes 12296 | tf_op jit(solution)/shard_map/ppermute | solution.py:456
  64.3 8.5 %collective-permute-start.21 = (f32[8,128]{1,0:T(8,128)S(1)}, f32[8,128]{1,0:T(8,128)S(1)}, u32[]{:S(2)}, u32[]{:S(2)}) collective-permute-start(f32[8,128]{1,0:T(8,128)S(1)} %add.22), channel_id=1, source_target_pairs={{0,20},{4,16},{8,28},{12,24},{16,4},{20,0},{24,12},{28,8},{1,21},{... | collective-permute-start | bytes 12296 | tf_op jit(solution)/shard_map/ppermute | solution.py:456
  69.1 3.8 %collective-permute-start.19 = (f32[8,128]{1,0:T(8,128)S(1)}, f32[8,128]{1,0:T(8,128)S(1)}, u32[]{:S(2)}, u32[]{:S(2)}) collective-permute-start(f32[8,128]{1,0:T(8,128)S(1)} %add.22), channel_id=1, source_target_pairs={{0,4},{4,0},{8,12},{12,8},{16,20},{20,16},{24,28},{28,24},{1,5},{5... | collective-permute-start | bytes 12296 | tf_op jit(solution)/shard_map/ppermute | solution.py:456
  (1 other events, 0.6 us)
where the time goes:
time: 74.7 us; the launch traced here: 73.4 us
  starting transfers between devices  33.8 us (45%)
  waiting for transfers between devices  21.8 us (29%)
  Pallas kernels  12.6 us (17%)
  local copies, waits for them, and re-layouts  4.28 us (6%)
  between operations  0.84 us (1%)
    ppermute x1, waiting for transfers between devices, middle_body(): far_around = lax.ppermute(packed(first, second), 'fib', inward[2])  9.26 us
    pallas_call x2, Pallas kernels, products(): pl.pallas_call(functools.partial(product_kernel, sizes, chunk, is_first),...  7.35 us
    ppermute x6, starting transfers between devices, middle_body(): lax.ppermute(part, 'fib', outward[m - 1])  6.51 us
    ppermute x6, waiting for transfers between devices, middle_body(): lax.ppermute(part, 'fib', outward[m - 1])  6.25 us
    ppermute x2, starting transfers between devices, middle_body(): near, mid = (lax.ppermute(flat, 'fib', pairs) for pairs in inward[:2])  5.66 us
    ppermute x1, starting transfers between devices, middle_body(): far_around = lax.ppermute(packed(first, second), 'fib', inward[2])  5.52 us
    ppermute x1, waiting for transfers between devices, middle_body(): found_first = lax.ppermute(found, PLANE, swap)  5.12 us
    ppermute x1, starting transfers between devices, middle_body(): far = lax.ppermute(later, 'fib', inward[2])  3.99 us
  transfers between devices with their start and end apart: 22, of which 6 were waited for; matrix products, arithmetic and copies ran while one was open for 0% of the time, Pallas kernels for 12%

commit v1 on v0

--- a/solution.py
+++ b/solution.py
@@ -425,7 +425,8 @@
     near_turned, mid_turned, far_turned = (
         turned_half(half.reshape(1), slab) for slab in (near, mid, far)
     )
-    found_second = lax.ppermute(found_first, PLANE, skip)
+    found_passed, _ = lax.optimization_barrier((found_first, own_second))
+    found_second = lax.ppermute(found_passed, PLANE, skip)
     first, second, *_ = lax.optimization_barrier((own_first, own_second, found_second))
     far_around = lax.ppermute(packed(first, second), "fib", inward[2])
     table = slot_table(groups, group_ref, counts, columns, found, found_first, found_second)

time: 74.7 us -> 78.6 us (1.052)
  waiting for transfers between devices: 21.8 us -> 29.2 us
  starting transfers between devices: 33.8 us -> 30.8 us
  Pallas kernels: 12.6 us -> 13.8 us
  local copies, waits for them, and re-layouts: 4.28 us -> 3.2 us
    ppermute x1, waiting for transfers between devices: 0.01 us -> 6.15 us  [middle_body(): own_second = lax.ppermute(own_passed, PLANE, skip)]
    ppermute x6, waiting for transfers between devices: 6.25 us -> 9.38 us  [middle_body(): lax.ppermute(part, 'fib', outward[m - 1])]
    ppermute x1, waiting for transfers between devices: 5.12 us -> 3.07 us  [middle_body(): found_first = lax.ppermute(found, PLANE, swap)]
    ppermute x4, starting transfers between devices: 2.79 us -> 1.16 us  [moved(): return lax.ppermute(array, PLANE, [(i, i ^ bits) for i in range(groups)])]
    ppermute x1, starting transfers between devices: 1.63 us -> 0.01 us  [middle_body(): found_second = lax.ppermute(found_passed, PLANE, skip)]
    ppermute x2, starting transfers between devices: 5.66 us -> 4.21 us  [middle_body(): near, mid = (lax.ppermute(flat, 'fib', pairs) for pairs in inward[:2])]
    ppermute x1, starting transfers between devices: 1.54 us -> 3 us  [middle_body(): own_first = lax.ppermute(own, PLANE, swap)]
    ppermute x1, starting transfers between devices: 5.52 us -> 6.62 us  [middle_body(): far_around = lax.ppermute(packed(first, second), 'fib', inward[2])]
  transfers between devices with their start and end apart: 22 -> 22, of which waited for: 6 -> 7; matrix products, arithmetic and copies ran while one was open for 0% -> 0% of each run, Pallas kernels for 12% -> 11%
where the time goes in v1:
time: 78.6 us; the launch traced here: 78 us
  starting transfers between devices  30.8 us (39%)
  waiting for transfers between devices  29.2 us (37%)
  Pallas kernels  13.8 us (18%)
  local copies, waits for them, and re-layouts  3.2 us (4%)
  between operations  0.87 us (1%)
    ppermute x1, waiting for transfers between devices, middle_body(): far_around = lax.ppermute(packed(first, second), 'fib', inward[2])  9.51 us
    ppermute x6, waiting for transfers between devices, middle_body(): lax.ppermute(part, 'fib', outward[m - 1])  9.38 us
    pallas_call x2, Pallas kernels, products(): pl.pallas_call(functools.partial(product_kernel, sizes, chunk, is_first),...  7.53 us
    ppermute x1, starting transfers between devices, middle_body(): far_around = lax.ppermute(packed(first, second), 'fib', inward[2])  6.62 us
    ppermute x6, starting transfers between devices, middle_body(): lax.ppermute(part, 'fib', outward[m - 1])  6.51 us
    ppermute x1, waiting for transfers between devices, middle_body(): own_second = lax.ppermute(own_passed, PLANE, skip)  6.15 us
    ppermute x2, starting transfers between devices, middle_body(): near, mid = (lax.ppermute(flat, 'fib', pairs) for pairs in inward[:2])  4.21 us
    ppermute x1, starting transfers between devices, middle_body(): far = lax.ppermute(later, 'fib', inward[2])  3.96 us
  transfers between devices with their start and end apart: 22, of which 7 were waited for; matrix products, arithmetic and copies ran while one was open for 0% of the time, Pallas kernels for 11%

profile of v1, /device:TPU:0, one launch (start us, length us, event | category | flops | bytes accessed | tf_op | source)
XLA Modules:
  0.0 78.0 jit_solution(12337346579991546389)
XLA Ops:
  0.6 1.6 %turn.4.refs_4_ = bf16[1152,128]{1,0:T(8,128)(2,1)S(1)} custom-call(s32[1]{0:T(128)} %bitcast.3.half_ref, bf16[2304,128]{1,0:T(8,128)(2,1)} %bitcast.4.in_ref.refs_0_), custom_call_target="tpu_custom_call" | custom-call | tf_op jit(solution)/shard_map/turn/pallas_call | solution.py:115
  2.2 3.0 %collective-permute-start.1 = (bf16[1152,128]{1,0:T(8,128)(2,1)S(1)}, bf16[1152,128]{1,0:T(8,128)(2,1)S(1)}, u32[]{:S(2)}, u32[]{:S(2)}) collective-permute-start(bf16[1152,128]{1,0:T(8,128)(2,1)S(1)} %turn.4.refs_4_), channel_id=1, source_target_pairs={{0,4},{4,0},{8,12},{12,8},{16,20},{20,16},{24,28},{28,24},{1,5},{5... | collective-permute-start | bytes 884744 | tf_op jit(solution)/shard_map/ppermute | solution.py:417
  5.2 3.5 %collective-permute-start.4 = (bf16[2304,128]{1,0:T(8,128)(2,1)}, bf16[2304,128]{1,0:T(8,128)(2,1)S(1)}, u32[]{:S(2)}, u32[]{:S(2)}) collective-permute-start(bf16[2304,128]{1,0:T(8,128)(2,1)} %bitcast.4.in_ref.refs_0_), channel_id=1, source_target_pairs={{0,1},{3,2},{4,5},{7,6},{8,9},{11,10},{12,13},{15,14},{16,17},{19,... | collective-permute-start | bytes 1769480 | tf_op jit(solution)/shard_map/ppermute | solution.py:412
  8.7 0.7 collective-permute-start.5
  10.1 0.6 find.1.own_ref
  11.4 3.1 %collective-permute-done.first_ref = s32[6,128]{1,0:T(8,128)S(1)} collective-permute-done((s32[6,128]{1,0:T(8,128)S(1)}, s32[6,128]{1,0:T(8,128)S(1)}, u32[]{:S(2)}, u32[]{:S(2)}) %collective-permute-start) | collective-permute-done | bytes 3104 | tf_op jit(solution)/shard_map/ppermute | solution.py:420
  14.5 6.1 %collective-permute-done.2.second_ref.refs_10_ = bf16[1152,128]{1,0:T(8,128)(2,1)S(1)} collective-permute-done((bf16[1152,128]{1,0:T(8,128)(2,1)S(1)}, bf16[1152,128]{1,0:T(8,128)(2,1)S(1)}, u32[]{:S(2)}, u32[]{:S(2)}) %collective-permute-start.2) | collective-permute-done | bytes 294944 | tf_op jit(solution)/shard_map/ppermute | solution.py:422
  20.6 4.0 %collective-permute-start.6 = (bf16[2304,128]{1,0:T(8,128)(2,1)}, bf16[2304,128]{1,0:T(8,128)(2,1)S(1)}, u32[]{:S(2)}, u32[]{:S(2)}) collective-permute-start(bf16[2304,128]{1,0:T(8,128)(2,1)} %bitcast.4.in_ref.refs_0_), channel_id=1, source_target_pairs={{0,2},{3,1},{4,6},{7,5},{8,10},{11,9},{12,14},{15,13},{16,18},{19,... | collective-permute-start | bytes 1769480 | tf_op jit(solution)/shard_map/ppermute | solution.py:424
  25.1 0.7 collective-permute-start.7
  26.3 1.4 %collective-permute-start.8 = (bf16[1152,128]{1,0:T(8,128)(2,1)S(1)}, bf16[1152,128]{1,0:T(8,128)(2,1)}, u32[]{:S(2)}, u32[]{:S(2)}) collective-permute-start(bf16[1152,128]{1,0:T(8,128)(2,1)S(1)} %turn.6.refs_6_), channel_id=1, source_target_pairs={{1,5},{2,6},{5,1},{6,2},{9,13},{10,14},{13,9},{14,10},{17,21},{18,... | collective-permute-start | bytes 884744 | tf_op jit(solution)/shard_map/ppermute | solution.py:407
  27.7 0.9 %pack.1 = bf16[2304,128]{1,0:T(8,128)(2,1)} custom-call(bf16[1152,128]{1,0:T(8,128)(2,1)S(1)} %collective-permute-done.1.first_ref.refs_7_, bf16[1152,128]{1,0:T(8,128)(2,1)S(1)} %collective-permute-done.2.second_ref.refs_10_), custom_call_target="tpu_custom_call" | custom-call | tf_op jit(solution)/shard_map/pack/pallas_call | solution.py:133
  28.5 6.6 %collective-permute-start.11 = (bf16[2304,128]{1,0:T(8,128)(2,1)}, bf16[2304,128]{1,0:T(8,128)(2,1)}, u32[]{:S(2)}, u32[]{:S(2)}) collective-permute-start(bf16[2304,128]{1,0:T(8,128)(2,1)} %pack.1), channel_id=1, source_target_pairs={{0,2},{3,1},{4,6},{7,5},{8,10},{11,9},{12,14},{15,13},{16,18},{19,... | collective-permute-start | bytes 1769480 | tf_op jit(solution)/shard_map/ppermute | solution.py:431
  35.1 1.4 %collective-permute-start.9 = (bf16[1152,128]{1,0:T(8,128)(2,1)S(1)}, bf16[1152,128]{1,0:T(8,128)(2,1)}, u32[]{:S(2)}, u32[]{:S(2)}) collective-permute-start(bf16[1152,128]{1,0:T(8,128)(2,1)S(1)} %collective-permute-done.7.refs_8_), channel_id=1, source_target_pairs={{25,1},{26,2},{13,5},{14,6},{1,9},{2,10},{21,13},{22,14},{9,17},{1... | collective-permute-start | bytes 884744 | tf_op jit(solution)/shard_map/ppermute | solution.py:409
  36.5 1.4 %collective-permute-start.10 = (bf16[1152,128]{1,0:T(8,128)(2,1)}, bf16[1152,128]{1,0:T(8,128)(2,1)}, u32[]{:S(2)}, u32[]{:S(2)}) collective-permute-start(bf16[1152,128]{1,0:T(8,128)(2,1)} %collective-permute-done.8.refs_9_), channel_id=1, source_target_pairs={{25,1},{26,2},{13,5},{14,6},{1,9},{2,10},{21,13},{22,14},{9,17},{1... | collective-permute-start | bytes 884744 | tf_op jit(solution)/shard_map/ppermute | solution.py:409
  38.0 0.7 copy-done.2
  38.7 0.7 copy-done.4
  39.3 0.7 copy-done.6
  41.1 9.5 %collective-permute-done.11.refs_13_ = bf16[2304,128]{1,0:T(8,128)(2,1)} collective-permute-done((bf16[2304,128]{1,0:T(8,128)(2,1)}, bf16[2304,128]{1,0:T(8,128)(2,1)}, u32[]{:S(2)}, u32[]{:S(2)}) %collective-permute-start.11) | collective-permute-done | bytes 589856 | tf_op jit(solution)/shard_map/ppermute | solution.py:431
  50.6 3.8 %products.2 = (bf16[592,128]{1,0:T(8,128)(2,1)S(1)}, bf16[592,128]{1,0:T(8,128)(2,1)S(1)}, bf16[592,128]{1,0:T(8,128)(2,1)S(1)}, bf16[592,128]{1,0:T(8,128)(2,1)S(1)}) custom-call(s32[4096]{0:T(1024)S(1)} %bitcast.13, s32[6]{0:T(128)S(1)} %stack.36.place_ref, bf16[2304,128]{1,0:T(8,128)(2,1)} %bitcast.4.in_ref.refs_0_, ...), custom_call_target="tpu_custom_call" | custom-call | flops 905969664 | bytes 4194304 | tf_op jit(solution)/shard_map/products/pallas_call | solution.py:311
  54.4 1.3 %collective-permute-start.12 = (bf16[592,128]{1,0:T(8,128)(2,1)S(1)}, bf16[592,128]{1,0:T(8,128)(2,1)S(1)}, u32[]{:S(2)}, u32[]{:S(2)}) collective-permute-start(bf16[592,128]{1,0:T(8,128)(2,1)S(1)} %get-tuple-element.21), channel_id=1, source_target_pairs={{2,0},{1,3},{6,4},{5,7},{10,8},{9,11},{14,12},{13,15},{18,16},{17,... | collective-permute-start | bytes 454664 | tf_op jit(solution)/shard_map/ppermute | solution.py:450
  55.7 1.3 %collective-permute-start.13 = (bf16[592,128]{1,0:T(8,128)(2,1)S(1)}, bf16[592,128]{1,0:T(8,128)(2,1)S(1)}, u32[]{:S(2)}, u32[]{:S(2)}) collective-permute-start(bf16[592,128]{1,0:T(8,128)(2,1)S(1)} %get-tuple-element.22), channel_id=1, source_target_pairs={{1,0},{2,3},{5,4},{6,7},{9,8},{10,11},{13,12},{14,15},{17,16},{18,... | collective-permute-start | bytes 454664 | tf_op jit(solution)/shard_map/ppermute | solution.py:450
  57.0 0.7 collective-permute-start.14
  57.7 3.7 %products.3 = (bf16[576,128]{1,0:T(8,128)(2,1)S(1)}, bf16[576,128]{1,0:T(8,128)(2,1)S(1)}, bf16[576,128]{1,0:T(8,128)(2,1)S(1)}, bf16[576,128]{1,0:T(8,128)(2,1)S(1)}) custom-call(s32[4096]{0:T(1024)S(1)} %bitcast.14, s32[6]{0:T(128)S(1)} %stack.36.place_ref, bf16[2304,128]{1,0:T(8,128)(2,1)} %bitcast.4.in_ref.refs_0_, ...), custom_call_target="tpu_custom_call" | custom-call | flops 905969664 | bytes 4194304 | tf_op jit(solution)/shard_map/products/pallas_call | solution.py:311
  61.4 1.3 %collective-permute-start.15 = (bf16[576,128]{1,0:T(8,128)(2,1)S(1)}, bf16[576,128]{1,0:T(8,128)(2,1)S(1)}, u32[]{:S(2)}, u32[]{:S(2)}) collective-permute-start(bf16[576,128]{1,0:T(8,128)(2,1)S(1)} %get-tuple-element.25), channel_id=1, source_target_pairs={{2,0},{1,3},{6,4},{5,7},{10,8},{9,11},{14,12},{13,15},{18,16},{17,... | collective-permute-start | bytes 442376 | tf_op jit(solution)/shard_map/ppermute | solution.py:450
  62.7 1.3 %collective-permute-start.16 = (bf16[576,128]{1,0:T(8,128)(2,1)S(1)}, bf16[576,128]{1,0:T(8,128)(2,1)S(1)}, u32[]{:S(2)}, u32[]{:S(2)}) collective-permute-start(bf16[576,128]{1,0:T(8,128)(2,1)S(1)} %get-tuple-element.26), channel_id=1, source_target_pairs={{1,0},{2,3},{5,4},{6,7},{9,8},{10,11},{13,12},{14,15},{17,16},{18,... | collective-permute-start | bytes 442376 | tf_op jit(solution)/shard_map/ppermute | solution.py:450
  64.0 0.7 collective-permute-start.17
  64.7 2.3 %collective-permute-done.13.refs_2_.near_ref = bf16[592,128]{1,0:T(8,128)(2,1)S(1)} collective-permute-done((bf16[592,128]{1,0:T(8,128)(2,1)S(1)}, bf16[592,128]{1,0:T(8,128)(2,1)S(1)}, u32[]{:S(2)}, u32[]{:S(2)}) %collective-permute-start.13) | collective-permute-done | bytes 151584 | tf_op jit(solution)/shard_map/ppermute | solution.py:450
  67.2 1.1 %collective-permute-done.18 = f32[8,128]{1,0:T(8,128)S(1)} collective-permute-done((f32[8,128]{1,0:T(8,128)S(1)}, f32[8,128]{1,0:T(8,128)S(1)}, u32[]{:S(2)}, u32[]{:S(2)}) %collective-permute-start.18) | collective-permute-done | bytes 4128 | tf_op jit(solution)/shard_map/ppermute | solution.py:457
  68.3 1.0 %collective-permute-start.20 = (f32[8,128]{1,0:T(8,128)S(1)}, f32[8,128]{1,0:T(8,128)S(1)}, u32[]{:S(2)}, u32[]{:S(2)}) collective-permute-start(f32[8,128]{1,0:T(8,128)S(1)} %add.22), channel_id=1, source_target_pairs={{0,16},{4,20},{8,24},{12,28},{16,0},{20,4},{24,8},{28,12},{1,17},{... | collective-permute-start | bytes 12296 | tf_op jit(solution)/shard_map/ppermute | solution.py:457
  69.3 4.0 %collective-permute-done.15.refs_5_ = bf16[576,128]{1,0:T(8,128)(2,1)S(1)} collective-permute-done((bf16[576,128]{1,0:T(8,128)(2,1)S(1)}, bf16[576,128]{1,0:T(8,128)(2,1)S(1)}, u32[]{:S(2)}, u32[]{:S(2)}) %collective-permute-start.15) | collective-permute-done | bytes 147488 | tf_op jit(solution)/shard_map/ppermute | solution.py:450
  73.3 3.1 %collective-permute-done.16.refs_6_ = bf16[576,128]{1,0:T(8,128)(2,1)S(1)} collective-permute-done((bf16[576,128]{1,0:T(8,128)(2,1)S(1)}, bf16[576,128]{1,0:T(8,128)(2,1)S(1)}, u32[]{:S(2)}, u32[]{:S(2)}) %collective-permute-start.16) | collective-permute-done | bytes 147488 | tf_op jit(solution)/shard_map/ppermute | solution.py:450
  76.4 1.0 %join.1 = bf16[6,3,128,128]{3,2,1,0:T(8,128)(2,1)} custom-call(s32[1]{0:T(128)} %bitcast.fib_ref, bf16[592,128]{1,0:T(8,128)(2,1)S(1)} %get-tuple-element.20.refs_0_.own_ref, bf16[592,128]{1,0:T(8,128)(2,1)S(1)} %collective-permute-done.12.refs_1_.far_ref, bf16[592,128]{1,0:T(8,128)(2,1)S(1)} %collective-permute-done.13.refs_2_.near_ref, ...), custom_call_target="tpu_custom_call" | custom-call | tf_op jit(solution)/shard_map/join/pallas_call | solution.py:380
  (42 shorter events, 4.2 us)
Async XLA Ops:
  2.2 12.3 %collective-permute-start.1 = (bf16[1152,128]{1,0:T(8,128)(2,1)S(1)}, bf16[1152,128]{1,0:T(8,128)(2,1)S(1)}, u32[]{:S(2)}, u32[]{:S(2)}) collective-permute-start(bf16[1152,128]{1,0:T(8,128)(2,1)S(1)} %turn.4.refs_4_), channel_id=1, source_target_pairs={{0,4},{4,0},{8,12},{12,8},{16,20},{20,16},{24,28},{28,24},{1,5},{5... | collective-permute-start | bytes 884744 | tf_op jit(solution)/shard_map/ppermute | solution.py:417
  5.2 19.4 %collective-permute-start.4 = (bf16[2304,128]{1,0:T(8,128)(2,1)}, bf16[2304,128]{1,0:T(8,128)(2,1)S(1)}, u32[]{:S(2)}, u32[]{:S(2)}) collective-permute-start(bf16[2304,128]{1,0:T(8,128)(2,1)} %bitcast.4.in_ref.refs_0_), channel_id=1, source_target_pairs={{0,1},{3,2},{4,5},{7,6},{8,9},{11,10},{12,13},{15,14},{16,17},{19,... | collective-permute-start | bytes 1769480 | tf_op jit(solution)/shard_map/ppermute | solution.py:412
  8.7 17.1 %collective-permute-start.5 = (bf16[2304,128]{1,0:T(8,128)(2,1)}, bf16[2304,128]{1,0:T(8,128)(2,1)S(1)}, u32[]{:S(2)}, u32[]{:S(2)}) collective-permute-start(bf16[2304,128]{1,0:T(8,128)(2,1)} %bitcast.4.in_ref.refs_0_), channel_id=1, source_target_pairs={{1,2},{2,1},{5,6},{6,5},{9,10},{10,9},{13,14},{14,13},{17,18},{18,... | collective-permute-start | bytes 1769480 | tf_op jit(solution)/shard_map/ppermute | solution.py:412
  9.4 0.7 copy-start
  9.5 0.7 copy-start.3
  10.1 0.6 copy-start.5
  10.8 3.7 %collective-permute-start = (s32[6,128]{1,0:T(8,128)S(1)}, s32[6,128]{1,0:T(8,128)S(1)}, u32[]{:S(2)}, u32[]{:S(2)}) collective-permute-start(s32[6,128]{1,0:T(8,128)S(1)} %find.1.own_ref), channel_id=1, source_target_pairs={{0,4},{4,0},{8,12},{12,8},{16,20},{20,16},{24,28},{28,24},{1,5},{5... | collective-permute-start | bytes 9224 | tf_op jit(solution)/shard_map/ppermute | solution.py:420
  14.5 6.1 %collective-permute-start.2 = (bf16[1152,128]{1,0:T(8,128)(2,1)S(1)}, bf16[1152,128]{1,0:T(8,128)(2,1)S(1)}, u32[]{:S(2)}, u32[]{:S(2)}) collective-permute-start(bf16[1152,128]{1,0:T(8,128)(2,1)S(1)} %collective-permute-done.1.first_ref.refs_7_), channel_id=1, source_target_pairs={{24,0},{12,4},{0,8},{20,12},{8,16},{28,20},{16,24},{4,28},{25,1},{... | collective-permute-start | bytes 884744 | tf_op jit(solution)/shard_map/ppermute | solution.py:422
  20.6 7.0 %collective-permute-start.3 = (s32[6,128]{1,0:T(8,128)S(1)}, s32[6,128]{1,0:T(8,128)S(1)}, u32[]{:S(2)}, u32[]{:S(2)}) collective-permute-start(s32[6,128]{1,0:T(8,128)S(1)} %collective-permute-done.first_ref), channel_id=1, source_target_pairs={{24,0},{12,4},{0,8},{20,12},{8,16},{28,20},{16,24},{4,28},{25,1},{... | collective-permute-start | bytes 9224 | tf_op jit(solution)/shard_map/ppermute | solution.py:429
  20.6 19.9 %collective-permute-start.6 = (bf16[2304,128]{1,0:T(8,128)(2,1)}, bf16[2304,128]{1,0:T(8,128)(2,1)S(1)}, u32[]{:S(2)}, u32[]{:S(2)}) collective-permute-start(bf16[2304,128]{1,0:T(8,128)(2,1)} %bitcast.4.in_ref.refs_0_), channel_id=1, source_target_pairs={{0,2},{3,1},{4,6},{7,5},{8,10},{11,9},{12,14},{15,13},{16,18},{19,... | collective-permute-start | bytes 1769480 | tf_op jit(solution)/shard_map/ppermute | solution.py:424
  25.1 10.1 %collective-permute-start.7 = (bf16[1152,128]{1,0:T(8,128)(2,1)S(1)}, bf16[1152,128]{1,0:T(8,128)(2,1)S(1)}, u32[]{:S(2)}, u32[]{:S(2)}) collective-permute-start(bf16[1152,128]{1,0:T(8,128)(2,1)S(1)} %turn.5.refs_5_), channel_id=1, source_target_pairs={{1,5},{2,6},{5,1},{6,2},{9,13},{10,14},{13,9},{14,10},{17,21},{18,... | collective-permute-start | bytes 884744 | tf_op jit(solution)/shard_map/ppermute | solution.py:407
  26.3 10.2 %collective-permute-start.8 = (bf16[1152,128]{1,0:T(8,128)(2,1)S(1)}, bf16[1152,128]{1,0:T(8,128)(2,1)}, u32[]{:S(2)}, u32[]{:S(2)}) collective-permute-start(bf16[1152,128]{1,0:T(8,128)(2,1)S(1)} %turn.6.refs_6_), channel_id=1, source_target_pairs={{1,5},{2,6},{5,1},{6,2},{9,13},{10,14},{13,9},{14,10},{17,21},{18,... | collective-permute-start | bytes 884744 | tf_op jit(solution)/shard_map/ppermute | solution.py:407
  27.7 0.9 %copy-start.1 = (s32[6,128]{1,0:T(8,128)}, s32[6,128]{1,0:T(8,128)S(1)}, u32[]{:S(2)}) copy-start(s32[6,128]{1,0:T(8,128)S(1)} %collective-permute-done.3.second_ref) | copy-start | bytes 9220
  28.5 22.1 %collective-permute-start.11 = (bf16[2304,128]{1,0:T(8,128)(2,1)}, bf16[2304,128]{1,0:T(8,128)(2,1)}, u32[]{:S(2)}, u32[]{:S(2)}) collective-permute-start(bf16[2304,128]{1,0:T(8,128)(2,1)} %pack.1), channel_id=1, source_target_pairs={{0,2},{3,1},{4,6},{7,5},{8,10},{11,9},{12,14},{15,13},{16,18},{19,... | collective-permute-start | bytes 1769480 | tf_op jit(solution)/shard_map/ppermute | solution.py:431
  35.1 5.9 %collective-permute-start.9 = (bf16[1152,128]{1,0:T(8,128)(2,1)S(1)}, bf16[1152,128]{1,0:T(8,128)(2,1)}, u32[]{:S(2)}, u32[]{:S(2)}) collective-permute-start(bf16[1152,128]{1,0:T(8,128)(2,1)S(1)} %collective-permute-done.7.refs_8_), channel_id=1, source_target_pairs={{25,1},{26,2},{13,5},{14,6},{1,9},{2,10},{21,13},{22,14},{9,17},{1... | collective-permute-start | bytes 884744 | tf_op jit(solution)/shard_map/ppermute | solution.py:409
  36.5 4.5 %collective-permute-start.10 = (bf16[1152,128]{1,0:T(8,128)(2,1)}, bf16[1152,128]{1,0:T(8,128)(2,1)}, u32[]{:S(2)}, u32[]{:S(2)}) collective-permute-start(bf16[1152,128]{1,0:T(8,128)(2,1)} %collective-permute-done.8.refs_9_), channel_id=1, source_target_pairs={{25,1},{26,2},{13,5},{14,6},{1,9},{2,10},{21,13},{22,14},{9,17},{1... | collective-permute-start | bytes 884744 | tf_op jit(solution)/shard_map/ppermute | solution.py:409
  38.0 0.7 copy-start.2
  38.6 0.7 copy-start.4
  39.3 0.7 copy-start.6
  54.4 9.6 %collective-permute-start.12 = (bf16[592,128]{1,0:T(8,128)(2,1)S(1)}, bf16[592,128]{1,0:T(8,128)(2,1)S(1)}, u32[]{:S(2)}, u32[]{:S(2)}) collective-permute-start(bf16[592,128]{1,0:T(8,128)(2,1)S(1)} %get-tuple-element.21), channel_id=1, source_target_pairs={{2,0},{1,3},{6,4},{5,7},{10,8},{9,11},{14,12},{13,15},{18,16},{17,... | collective-permute-start | bytes 454664 | tf_op jit(solution)/shard_map/ppermute | solution.py:450
  55.7 11.3 %collective-permute-start.13 = (bf16[592,128]{1,0:T(8,128)(2,1)S(1)}, bf16[592,128]{1,0:T(8,128)(2,1)S(1)}, u32[]{:S(2)}, u32[]{:S(2)}) collective-permute-start(bf16[592,128]{1,0:T(8,128)(2,1)S(1)} %get-tuple-element.22), channel_id=1, source_target_pairs={{1,0},{2,3},{5,4},{6,7},{9,8},{10,11},{13,12},{14,15},{17,16},{18,... | collective-permute-start | bytes 454664 | tf_op jit(solution)/shard_map/ppermute | solution.py:450
  57.0 10.0 %collective-permute-start.14 = (bf16[592,128]{1,0:T(8,128)(2,1)S(1)}, bf16[592,128]{1,0:T(8,128)(2,1)S(1)}, u32[]{:S(2)}, u32[]{:S(2)}) collective-permute-start(bf16[592,128]{1,0:T(8,128)(2,1)S(1)} %get-tuple-element.23), channel_id=1, source_target_pairs={{2,1},{1,2},{6,5},{5,6},{10,9},{9,10},{14,13},{13,14},{18,17},{17,... | collective-permute-start | bytes 454664 | tf_op jit(solution)/shard_map/ppermute | solution.py:450
  61.4 11.9 %collective-permute-start.15 = (bf16[576,128]{1,0:T(8,128)(2,1)S(1)}, bf16[576,128]{1,0:T(8,128)(2,1)S(1)}, u32[]{:S(2)}, u32[]{:S(2)}) collective-permute-start(bf16[576,128]{1,0:T(8,128)(2,1)S(1)} %get-tuple-element.25), channel_id=1, source_target_pairs={{2,0},{1,3},{6,4},{5,7},{10,8},{9,11},{14,12},{13,15},{18,16},{17,... | collective-permute-start | bytes 442376 | tf_op jit(solution)/shard_map/ppermute | solution.py:450
  62.7 13.7 %collective-permute-start.16 = (bf16[576,128]{1,0:T(8,128)(2,1)S(1)}, bf16[576,128]{1,0:T(8,128)(2,1)S(1)}, u32[]{:S(2)}, u32[]{:S(2)}) collective-permute-start(bf16[576,128]{1,0:T(8,128)(2,1)S(1)} %get-tuple-element.26), channel_id=1, source_target_pairs={{1,0},{2,3},{5,4},{6,7},{9,8},{10,11},{13,12},{14,15},{17,16},{18,... | collective-permute-start | bytes 442376 | tf_op jit(solution)/shard_map/ppermute | solution.py:450
  64.0 12.4 %collective-permute-start.17 = (bf16[576,128]{1,0:T(8,128)(2,1)S(1)}, bf16[576,128]{1,0:T(8,128)(2,1)S(1)}, u32[]{:S(2)}, u32[]{:S(2)}) collective-permute-start(bf16[576,128]{1,0:T(8,128)(2,1)S(1)} %get-tuple-element.27), channel_id=1, source_target_pairs={{2,1},{1,2},{6,5},{5,6},{10,9},{9,10},{14,13},{13,14},{18,17},{17,... | collective-permute-start | bytes 442376 | tf_op jit(solution)/shard_map/ppermute | solution.py:450
  67.1 1.2 %collective-permute-start.18 = (f32[8,128]{1,0:T(8,128)S(1)}, f32[8,128]{1,0:T(8,128)S(1)}, u32[]{:S(2)}, u32[]{:S(2)}) collective-permute-start(f32[8,128]{1,0:T(8,128)S(1)} %add.31), channel_id=1, source_target_pairs={{0,8},{4,12},{8,0},{12,4},{16,24},{20,28},{24,16},{28,20},{1,9},{5... | collective-permute-start | bytes 12296 | tf_op jit(solution)/shard_map/ppermute | solution.py:457
  68.3 9.1 %collective-permute-start.20 = (f32[8,128]{1,0:T(8,128)S(1)}, f32[8,128]{1,0:T(8,128)S(1)}, u32[]{:S(2)}, u32[]{:S(2)}) collective-permute-start(f32[8,128]{1,0:T(8,128)S(1)} %add.22), channel_id=1, source_target_pairs={{0,16},{4,20},{8,24},{12,28},{16,0},{20,4},{24,8},{28,12},{1,17},{... | collective-permute-start | bytes 12296 | tf_op jit(solution)/shard_map/ppermute | solution.py:457
  69.3 8.1 %collective-permute-start.21 = (f32[8,128]{1,0:T(8,128)S(1)}, f32[8,128]{1,0:T(8,128)S(1)}, u32[]{:S(2)}, u32[]{:S(2)}) collective-permute-start(f32[8,128]{1,0:T(8,128)S(1)} %add.22), channel_id=1, source_target_pairs={{0,20},{4,16},{8,28},{12,24},{16,4},{20,0},{24,12},{28,8},{1,21},{... | collective-permute-start | bytes 12296 | tf_op jit(solution)/shard_map/ppermute | solution.py:457
  73.3 4.1 %collective-permute-start.19 = (f32[8,128]{1,0:T(8,128)S(1)}, f32[8,128]{1,0:T(8,128)S(1)}, u32[]{:S(2)}, u32[]{:S(2)}) collective-permute-start(f32[8,128]{1,0:T(8,128)S(1)} %add.22), channel_id=1, source_target_pairs={{0,4},{4,0},{8,12},{12,8},{16,20},{20,16},{24,28},{28,24},{1,5},{5... | collective-permute-start | bytes 12296 | tf_op jit(solution)/shard_map/ppermute | solution.py:457
